TPU v7x, 256 devices: a whole 4x4x8 slice. The times are simulated.
256 devices in a mesh: row: 8 (over y_hi, x), col: 16 (over z, y_lo), sea: 2 (over core).
Axes of the slice: x: 4, y: 4 (y_hi: 2, y_lo: 2; y = y_hi * 2 + y_lo), z: 8, core: 2. Of those that a mesh axis runs over, the one named last changes fastest.
Arguments:
- kernel: bfloat16 [16, 8, 768, 6144], P(None, None, 'col', 'row'), may hold values from -0.01953125 to 0.01953125
- history: bfloat16 [15, 8, 768, 512], P(None, None, 'col', 'sea'), may hold values from -6 to 6
- displacement: float32 [6144, 512], P(('row', 'col'), 'sea'), may hold values from -6 to 6
- velocity: float32 [6144, 512], P(('row', 'col'), 'sea'), may hold values from -6 to 6
- acceleration: float32 [6144, 512], P(('row', 'col'), 'sea'), may hold values from -6 to 6
- excitation: float32 [3, 6144, 512], P(None, ('row', 'col'), 'sea'), may hold values from -6 to 6
- solve_inverse: float32 [1024, 6, 6], P(('row', 'col')), may hold values from -2.5 to 2.5
- stiffness: float32 [1024, 6, 6], P(('row', 'col')), may hold values from -2.5 to 2.5
- owned: int32 [1024], replicated, may hold values from 0 to 1023, as said below
- links: int32 [1024, 16], P(('row', 'col')), may hold values from 0 to 16383, as said below
- arms: float32 [1024, 3, 16], P(('row', 'col')), may hold values from -1 to 1
Outputs:
- final_velocity: float32 [6144, 512], P(('row', 'col'), 'sea')
- deck_gaps: float32 [1024, 16, 3, 512], P(('row', 'col'), None, None, 'sea')
Inputs may be any that keep to these rules, and one draw needn't show every extreme that they name: `owned`: A permutation of the 1024 modules. Module m has its modes on the grid device m // 8 (row-major over row, col); its owner has the same col. The modules that one device sends to one owner number at most 2, exactly 2 wherever any are sent, and their list positions differ modulo 2. `links`: the partner point lies on another module listed to the same owner.
All inputs are finite; a program needn't handle non-finite values.
Results may differ from a plain program's by a relative error of at most 0.00037.
Values may be sent and summed in bfloat16 or wider, within the bound.
A program may use at most 128 MiB of HBM per device.

v0:
```python
import jax
import jax.numpy as jnp
from jax import lax
from jax.sharding import PartitionSpec as P

POINTS = 16
STEPS = 3


DT = 0.5
QUARTER = DT * DT / 4.0


def blocks(matrix, vector):
    return jnp.einsum("mab,mbr->mar", matrix, vector, precision=lax.Precision.HIGHEST)


def newmark(
    displacement, velocity, acceleration, force_now, excitation_now, solve_inverse, stiffness
):
    block_shape = (displacement.shape[0] // 6, 6, displacement.shape[1])
    predicted = displacement + DT * velocity + QUARTER * acceleration
    load_total = (
        excitation_now
        - force_now
        - blocks(stiffness, predicted.reshape(block_shape)).reshape(displacement.shape)
    )
    accel_next = blocks(solve_inverse, load_total.reshape(block_shape)).reshape(displacement.shape)
    return (
        predicted + QUARTER * accel_next,
        velocity + 0.5 * DT * (acceleration + accel_next),
        accel_next,
    )


def deck_motion(motion, levers):
    moving = motion[:, 0:3, None, :]
    turning = motion[:, 3:6, None, :]
    arm_all = levers[:, :, :, None]
    surge_motion = moving[:, 0] + turning[:, 1] * arm_all[:, 2] - turning[:, 2] * arm_all[:, 1]
    sway_motion = moving[:, 1] + turning[:, 2] * arm_all[:, 0] - turning[:, 0] * arm_all[:, 2]
    heave_motion = moving[:, 2] + turning[:, 0] * arm_all[:, 1] - turning[:, 1] * arm_all[:, 0]
    return jnp.stack([surge_motion, sway_motion, heave_motion], axis=2)


def body(
    kernel,
    history,
    displacement,
    velocity,
    acceleration,
    excitation,
    solve_inverse,
    stiffness,
    owned,
    links,
    arms,
):
    lag_count = kernel.shape[0]
    row_total = lax.axis_size("row")
    col_total = lax.axis_size("col")
    slab_rows = velocity.shape[0]
    block_rows = kernel.shape[3]
    module_count = slab_rows // 6
    window = history
    kernel_flat = kernel.reshape(-1, block_rows)
    for step_index in range(STEPS):
        newest = lax.all_gather(velocity.astype(jnp.bfloat16), "row", axis=0, tiled=True)
        newest = newest.reshape(1, row_total, slab_rows, newest.shape[1])
        window = jnp.concatenate([newest, window[: lag_count - 1]], axis=0)
        window_flat = window.reshape(kernel_flat.shape[0], -1)
        force_now = lax.psum_scatter(
            lax.dot_general(
                kernel_flat,
                window_flat,
                (((0,), (0,)), ((), ())),
                preferred_element_type=jnp.float32,
            ),
            "col",
            scatter_dimension=0,
            tiled=True,
        )
        displacement, velocity, acceleration = newmark(
            displacement,
            velocity,
            acceleration,
            force_now,
            excitation[step_index],
            solve_inverse,
            stiffness,
        )
    motion = displacement.reshape(module_count, 6, -1)
    grid_index = lax.axis_index("row") * col_total + lax.axis_index("col")
    owned_here = lax.dynamic_slice_in_dim(owned, grid_index * module_count, module_count, 0)
    home_rows = owned_here // (col_total * module_count)
    capacity = 2 * module_count // row_total
    local_ids = grid_index * module_count + jnp.arange(module_count, dtype=jnp.int32)
    list_range = jnp.arange(owned.shape[0], dtype=jnp.int32)
    positions = jnp.sum(
        jnp.where(owned[None, :] == local_ids[:, None], list_range[None, :], 0), axis=1
    )
    targets = (
        positions // (col_total * module_count) * capacity + positions % module_count % capacity
    )
    routing = (
        targets[None, :] == jnp.arange(row_total * capacity, dtype=jnp.int32)[:, None]
    ).astype(jnp.float32)
    outgoing = jnp.einsum("sm,mar->sar", routing, motion, precision=lax.Precision.HIGHEST).reshape(
        row_total, capacity, 6, -1
    )
    arrived = lax.all_to_all(outgoing, "row", split_axis=0, concat_axis=0, tiled=True).reshape(
        row_total * capacity, 6, -1
    )
    slot_index = jnp.arange(module_count, dtype=jnp.int32) % capacity
    owned_motion = jnp.take(arrived, home_rows * capacity + slot_index, axis=0)
    points = deck_motion(owned_motion, arms).reshape(module_count * POINTS, 3, -1)
    local_links = (links - grid_index * module_count * POINTS).reshape(-1)
    partner = jnp.take(points, local_links, axis=0)
    deck_gaps = (points - partner).reshape(module_count, POINTS, 3, -1)
    return (velocity, deck_gaps)


def solution(mesh):
    placed = (
        P(None, None, "col", "row"),
        P(None, None, "col", "sea"),
        P(("row", "col"), "sea"),
        P(("row", "col"), "sea"),
        P(("row", "col"), "sea"),
        P(None, ("row", "col"), "sea"),
        P(("row", "col"), None, None),
        P(("row", "col"), None, None),
        P(),
        P(("row", "col"), None),
        P(("row", "col"), None, None),
    )
    return jax.shard_map(
        body,
        mesh=mesh,
        in_specs=placed,
        out_specs=(P(("row", "col"), "sea"), P(("row", "col"), None, None, "sea")),
        check_vma=False,
    )
```

profile of v0, /device:TPU:2, one launch (start us, length us, event | category | flops | bytes accessed | tf_op | source)
XLA Modules:
  0.0 378.5 jit_solution(11167240367918859943)
XLA Ops:
  7.2 0.9 fusion.48
  8.1 34.6 %all_gather.9 = bf16[384,256]{1,0:T(8,128)(2,1)S(1)} all-gather(bf16[48,256]{1,0:T(8,128)(2,1)S(1)} %get-tuple-element.25), channel_id=1, replica_groups=mesh['row'=8,'col'=16,'sea'=2] {'row'}, dimensions={0}, use_global_device_ids=true | all-gather | bytes 221184 | tf_op jit(solution)/shard_map/all_gather | solution.py:68
  42.7 7.3 %fusion.14 = f32[768,256]{0,1:T(8,128)S(1)} fusion(bf16[16,8,48,768]{3,2,1,0:T(8,128)(2,1)} %param.11, bf16[15,8,48,256]{3,2,1,0:T(8,128)(2,1)} %param.12, bf16[1,8,48,256]{3,2,1,0:T(8,128)(2,1)S(1)} %bitcast.112), kind=kOutput, calls=%fused_computation.17 | convolution fusion | flops 2417491968 | bytes 13369344 | tf_op jit(solution)/shard_map/dot_general | solution.py:73
  50.0 1.2 copy.99
  51.3 0.2 convolution_bitcast_fusion.5
  51.5 73.3 %reduce-scatter.10.cloned.1.call-done = f32[48,256]{1,0:T(8,128)} async-done(((f32[768,256]{1,0:T(8,128)}), f32[48,256]{1,0:T(8,128)}) %reduce-scatter.10.cloned.1.call-update) | async-done | bytes 49168 | tf_op jit(solution)/shard_map/reduce_scatter | solution.py:72
  124.7 0.8 fusion.27
  125.6 0.2 convolution_bitcast_fusion.4
  125.8 34.0 %all_gather.10 = bf16[384,256]{1,0:T(8,128)(2,1)S(1)} all-gather(bf16[48,256]{1,0:T(8,128)(2,1)S(1)} %get-tuple-element.16), channel_id=1, replica_groups=mesh['row'=8,'col'=16,'sea'=2] {'row'}, dimensions={0}, use_global_device_ids=true | all-gather | bytes 221184 | tf_op jit(solution)/shard_map/all_gather | solution.py:68
  159.8 7.2 %fusion.17 = f32[768,256]{0,1:T(8,128)S(1)} fusion(bf16[16,8,48,768]{3,2,1,0:T(8,128)(2,1)} %param.11, bf16[15,8,48,256]{3,2,1,0:T(8,128)(2,1)} %param.12, bf16[1,8,48,256]{3,2,1,0:T(8,128)(2,1)S(1)} %bitcast.113, bf16[1,8,48,256]{3,2,1,0:T(8,128)(2,1)S(1)} %bitcast.115), kind=kOutput, calls=%fused_computation.18 | convolution fusion | flops 2419064832 | bytes 13565952 | tf_op jit(solution)/shard_map/dot_general | solution.py:73
  167.0 1.2 copy.101
  168.3 0.2 convolution_bitcast_fusion.3
  168.5 69.3 %reduce-scatter.12.cloned.1.call-done = f32[48,256]{1,0:T(8,128)} async-done(((f32[768,256]{1,0:T(8,128)}), f32[48,256]{1,0:T(8,128)}) %reduce-scatter.12.cloned.1.call-update) | async-done | bytes 49168 | tf_op jit(solution)/shard_map/reduce_scatter | solution.py:72
  237.7 0.8 fusion.26
  238.6 0.2 convolution_bitcast_fusion.2
  238.8 34.0 %all_gather.11 = bf16[384,256]{1,0:T(8,128)(2,1)S(1)} all-gather(bf16[48,256]{1,0:T(8,128)(2,1)S(1)} %get-tuple-element.14), channel_id=1, replica_groups=mesh['row'=8,'col'=16,'sea'=2] {'row'}, dimensions={0}, use_global_device_ids=true | all-gather | bytes 221184 | tf_op jit(solution)/shard_map/all_gather | solution.py:68
  272.8 7.1 %fusion.20 = f32[768,256]{0,1:T(8,128)S(1)} fusion(bf16[16,8,48,768]{3,2,1,0:T(8,128)(2,1)} %param.11, bf16[1,8,48,256]{3,2,1,0:T(8,128)(2,1)S(1)} %bitcast.116, bf16[15,8,48,256]{3,2,1,0:T(8,128)(2,1)} %param.12, bf16[1,8,48,256]{3,2,1,0:T(8,128)(2,1)S(1)} %bitcast.114, bf16[1,8,48,256]{3,2,1,0:T(8,128)(2,1)S(1)} %bitcast.117), kind=kOutput, calls=%fused_computation.19 | convolution fusion | flops 2420637696 | bytes 13762560 | tf_op jit(solution)/shard_map/dot_general | solution.py:73
  279.9 1.2 copy.103
  281.1 0.1 mul.280
  281.2 0.1 mul.285
  281.3 0.1 mul.288
  281.4 0.1 reshape.520
  281.5 0.1 compare_and_fusion.1
  281.6 0.2 select_reduce_fusion
  281.9 0.2 convolution_bitcast_fusion.1
  282.1 68.7 %reduce-scatter.14.cloned.1.call-done = f32[48,256]{1,0:T(8,128)} async-done(((f32[768,256]{1,0:T(8,128)}), f32[48,256]{1,0:T(8,128)}) %reduce-scatter.14.cloned.1.call-update) | async-done | bytes 49168 | tf_op jit(solution)/shard_map/reduce_scatter | solution.py:72
  350.8 0.8 fusion.25
  351.6 0.2 convolution_bitcast_fusion
  351.8 0.6 multiply_add_fusion
  352.4 0.2 fusion.23
  352.7 0.7 copy.89
  353.4 7.0 %all-to-all-start = ((f32[8,2,6,256]{3,1,2,0:T(2,128)}), f32[8,2,6,256]{3,1,2,0:T(2,128)S(1)}, u32[]{:S(2)}, u32[]{:S(2)}) async-start(f32[8,2,6,256]{3,1,2,0:T(2,128)} %copy.89), calls=%async_computation | async-start | bytes 196608 | tf_op jit(solution)/shard_map/all_to_all | solution.py:111
  360.4 6.7 %all-to-all-done = f32[8,2,6,256]{3,1,2,0:T(2,128)S(1)} async-done(((f32[8,2,6,256]{3,1,2,0:T(2,128)}), f32[8,2,6,256]{3,1,2,0:T(2,128)S(1)}, u32[]{:S(2)}, u32[]{:S(2)}) %all-to-all-start) | async-done | bytes 98336 | tf_op jit(solution)/shard_map/all_to_all | solution.py:111
  367.1 0.6 gather_fusion
  367.7 0.1 broadcast_select_fusion
  367.9 0.1 add.259
  368.0 0.1 add.262
  368.2 0.1 add.265
  368.4 0.1 mul.279
  368.5 0.1 mul.284
  368.7 0.1 mul.292
  368.8 0.7 multiply_subtract_fusion.2
  369.6 0.3 pad_maximum_fusion.4
  369.9 0.9 gather_fusion.1
  370.8 0.1 copy.92
  370.9 0.1 multiply_subtract_fusion.5
  371.0 0.1 maximum_subtract_fusion
  371.2 0.8 copy.93
  (61 shorter events, 0.6 us)
Async XLA Ops:
  7.2 44.1 %copy-start = (f32[8,6,6]{2,0,1:T(8,128)S(1)}, f32[8,6,6]{2,0,1:T(8,128)}, u32[]{:S(2)}) copy-start(f32[8,6,6]{2,0,1:T(8,128)} %param.18) | copy-start | bytes 3460
  7.2 117.5 %reduce-scatter.10.cloned.1.call-start = ((), (), s32[]{:S(2)}) async-start(), calls=%async_computation.4 | async-start | bytes 835584 | tf_op jit(solution)/shard_map/reduce_scatter | solution.py:72
  42.7 82.0 %copy-start.4 = (f32[3,48,256]{2,1,0:T(8,128)S(1)}, f32[3,48,256]{2,1,0:T(8,128)}, u32[]{:S(2)}) copy-start(f32[3,48,256]{2,1,0:T(8,128)} %param.16) | copy-start | bytes 442372
  42.7 82.9 %copy-start.3 = (f32[8,6,6]{2,0,1:T(8,128)S(1)}, f32[8,6,6]{2,0,1:T(8,128)}, u32[]{:S(2)}) copy-start(f32[8,6,6]{2,0,1:T(8,128)} %param.17) | copy-start | bytes 3460
  50.0 75.8 %copy-start.1 = (f32[48,256]{1,0:T(8,128)S(1)}, f32[48,256]{1,0:T(8,128)}, u32[]{:S(2)}) copy-start(f32[48,256]{1,0:T(8,128)} %param.14) | copy-start | bytes 147460
  50.0 75.8 %copy-start.2 = (f32[48,256]{1,0:T(8,128)S(1)}, f32[48,256]{1,0:T(8,128)}, u32[]{:S(2)}) copy-start(f32[48,256]{1,0:T(8,128)} %param.15) | copy-start | bytes 147460
  51.2 186.6 %reduce-scatter.12.cloned.1.call-start = ((), (), s32[]{:S(2)}) async-start(), calls=%async_computation.5 | async-start | bytes 835584 | tf_op jit(solution)/shard_map/reduce_scatter | solution.py:72
  159.8 8.4 %copy-start.5 = (f32[8,3,16]{2,0,1:T(8,128)S(1)}, f32[8,3,16]{2,0,1:T(8,128)}, u32[]{:S(2)}) copy-start(f32[8,3,16]{2,0,1:T(8,128)} %param.21) | copy-start | bytes 4612
  168.2 182.6 %reduce-scatter.14.cloned.1.call-start = ((), (), s32[]{:S(2)}) async-start(), calls=%async_computation.6 | async-start | bytes 835584 | tf_op jit(solution)/shard_map/reduce_scatter | solution.py:72
  272.8 8.3 %copy-start.7 = (s32[8,16]{1,0:T(8,128)S(1)}, s32[8,16]{1,0:T(8,128)}, u32[]{:S(2)}) copy-start(s32[8,16]{1,0:T(8,128)} %param.20) | copy-start | bytes 1540
  272.8 8.7 %copy-start.6 = (s32[1024]{0:T(1024)S(1)}, s32[1024]{0:T(1024)}, u32[]{:S(2)}) copy-start(s32[1024]{0:T(1024)} %param.19) | copy-start | bytes 12292
  353.4 13.7 %all-to-all-start = ((f32[8,2,6,256]{3,1,2,0:T(2,128)}), f32[8,2,6,256]{3,1,2,0:T(2,128)S(1)}, u32[]{:S(2)}, u32[]{:S(2)}) async-start(f32[8,2,6,256]{3,1,2,0:T(2,128)} %copy.89), calls=%async_computation | async-start | bytes 196608 | tf_op jit(solution)/shard_map/all_to_all | solution.py:111
Sparse Core Ops, SparseCore 0:
  51.3 73.3 reduce-scatter.9
  168.3 69.3 reduce-scatter.11
  281.2 69.4 reduce-scatter.13
where the time goes:
time: 379 us; the launch traced here: 378 us
  waiting for transfers between devices  218 us (58%)
  blocking collectives  103 us (27%)
  matrix products  22.9 us (6%)
  between operations  14.3 us (4%)
  local copies, waits for them, and re-layouts  7.9 us (2%)
  starting transfers between devices  7.09 us (2%)
  other arithmetic  5.75 us (2%)
    reduce_scatter x3, waiting for transfers between devices, body(): lax.psum_scatter(lax.dot_general(kernel_flat, window_flat, (((0,), (0,)),...  211 us
    all_gather x3, blocking collectives, body(): lax.all_gather(velocity.astype(jnp.bfloat16), 'row', axis=0, tiled=True)  103 us
    dot_general x3, matrix products, body(): lax.dot_general(kernel_flat, window_flat, (((0,), (0,)), ((), ())), prefe...  21.6 us
  transfers between devices with their start and end apart: 4, of which 4 were waited for; matrix products, arithmetic and copies ran while one was open for 0% of the time, Pallas kernels for 0%

commit v1 on v0

v1 whole, which is shorter than its diff:
```python
import functools

import jax
import jax.numpy as jnp
from jax import lax
from jax.experimental import pallas as pl
from jax.experimental.pallas import tpu as pltpu
from jax.sharding import PartitionSpec as P

POINTS = 16
STEPS = 3
SLOTS = 2
LANE_ROWS = 16

DT = 0.5
QUARTER = DT * DT / 4.0
MESH = pl.DeviceIdType.MESH
EXACT = lax.Precision.HIGHEST


def iota(shape, dim):
    return lax.broadcasted_iota(jnp.int32, shape, dim)


def f32(mask):
    return jnp.where(mask, 1.0, 0.0).astype(jnp.float32)


def dot(a, b, precision=None):
    return lax.dot_general(
        a, b, (((1,), (0,)), ((), ())), precision=precision, preferred_element_type=jnp.float32
    )


def dot_nt(a, b, precision=None):
    return lax.dot_general(
        a, b, (((1,), (1,)), ((), ())), precision=precision, preferred_element_type=jnp.float32
    )


def block_diagonal(ref, modules):
    size = 6 * modules
    rows = []
    for m in range(modules):
        place = f32(iota((6, size), 1) == iota((6, size), 0) + 6 * m)
        rows.append(dot(ref[m], place, EXACT))
    return jnp.concatenate(rows, axis=0)


def routing_matrix(owned, base, modules):
    n_row, lanes = owned.shape
    lane = iota((n_row, lanes), 1)
    column = iota((n_row, modules), 1)
    out_rows = n_row * LANE_ROWS
    spread = f32(iota((modules, 6 * modules), 1) // 6 == iota((modules, 6 * modules), 0))
    total = jnp.zeros((out_rows, 6 * modules), jnp.float32)
    for slot in range(SLOTS):
        hit = jnp.zeros((n_row, modules), jnp.float32)
        for m in range(modules):
            here = f32((owned == base + m) & (lane % SLOTS == slot))
            hit = jnp.where(column == m, jnp.sum(here, axis=1, keepdims=True), hit)
        r = iota((out_rows, n_row), 0)
        lift = f32(
            (r // LANE_ROWS == iota((out_rows, n_row), 1))
            & (r % LANE_ROWS >= 6 * slot)
            & (r % LANE_ROWS < 6 * slot + 6)
        )
        wide = dot(dot(lift, hit), spread)
        rr = iota((out_rows, 6 * modules), 0) % LANE_ROWS - 6 * slot
        total = total + jnp.where(rr == iota((out_rows, 6 * modules), 1) % 6, wide, 0.0)
    return total


def choice_matrix(owned, row, col, home_size, modules):
    n_row, lanes = owned.shape
    home = owned // home_size
    mine = jnp.sum(jnp.where(iota((n_row, lanes), 0) == row, home, 0), axis=0, keepdims=True)
    per_lane = f32(iota((n_row, lanes), 0) == mine)
    size = 6 * modules
    pick = f32(iota((size, lanes), 1) == col * modules + iota((size, lanes), 0) // 6)
    by_row = dot_nt(pick, per_lane)
    out = n_row * LANE_ROWS
    widen = f32(iota((n_row, out), 1) // LANE_ROWS == iota((n_row, out), 0))
    wide = dot(by_row, widen)
    i = iota((size, out), 0)
    fits = iota((size, out), 1) % LANE_ROWS == 6 * (i // 6 % SLOTS) + i % 6
    return jnp.where(fits, wide, 0.0)


def gap_matrix(links_ref, arms_ref, first_point, modules):
    rows, size = 3 * POINTS, 6 * modules
    by_point = f32(iota((rows, POINTS), 0) // 3 == iota((rows, POINTS), 1))
    levers = [dot_nt(by_point, arms_ref[t], EXACT) for t in range(modules)]
    lane = iota((rows, size), 1)
    comp = iota((rows, size), 0) % 3
    mode = lane % 6
    form = f32(mode == comp)
    for d in range(3):
        along = jnp.zeros((rows, size), jnp.float32)
        for t in range(modules):
            along = jnp.where(lane // 6 == t, levers[t][:, d : d + 1], along)
        plus = mode == 3 + (comp + 1) % 3
        minus = mode == 3 + (comp + 2) % 3
        form = form + jnp.where(plus & (d == (comp + 2) % 3), along, 0.0)
        form = form - jnp.where(minus & (d == (comp + 1) % 3), along, 0.0)
    local = (links_ref[...] - first_point).astype(jnp.float32)
    partner = dot_nt(by_point, local, EXACT).astype(jnp.int32)
    wide = iota((rows, rows), 1)
    out = []
    for t in range(modules):
        met = partner[:, t : t + 1]
        pick = f32((met % POINTS == wide // 3) & (wide % 3 == iota((rows, rows), 0) % 3))
        other = dot(pick, form, EXACT)
        out.append(
            jnp.where(lane // 6 == t, form, 0.0) - jnp.where(lane // 6 == met // POINTS, other, 0.0)
        )
    return jnp.concatenate(out, axis=0)


def steps_kernel(
    n_row, n_col, lags, groups,
    kernel_hbm, history_hbm, x_hbm, v_hbm, a_hbm, exc_hbm, solve_hbm, stiff_hbm, owned_hbm, links_hbm, arms_hbm,
    v_out, deck_out,
    kern, hist, hist_t, x, v, a, exc, solve, stiff, owned, links, arms,
    k_t, acc, base_force, force, newest, window, received, outgoing, arrived, gaps, routing,
    local_sem, ag_send, ag_recv, rs_send, rs_recv, ex_send, ex_recv,
):
    row, col = lax.axis_index("row"), lax.axis_index("col")
    slab, reals = v.shape
    modules = slab // 6
    depth = n_row * slab
    block = n_col * slab
    grid_index = row * n_col + col

    sems = iter(range(64))

    def fetch(src, dst):
        copy = pltpu.make_async_copy(src, dst, local_sem.at[next(sems)])
        copy.start()
        return copy

    get_v = fetch(v_hbm, v)
    get_first = fetch(kernel_hbm.at[pl.ds(0, 1)], kern.at[pl.ds(0, 1)])
    get_groups = []
    for first, last in groups:
        get_groups.append(
            (
                fetch(history_hbm.at[pl.ds(first - 1, last - first)], hist.at[pl.ds(first - 1, last - first)]),
                fetch(kernel_hbm.at[pl.ds(first, last - first)], kern.at[pl.ds(first, last - first)]),
            )
        )
    get_state = [fetch(x_hbm, x), fetch(a_hbm, a), fetch(exc_hbm, exc), fetch(solve_hbm, solve), fetch(stiff_hbm, stiff)]
    get_tables = [fetch(owned_hbm, owned), fetch(links_hbm, links), fetch(arms_hbm, arms)]

    row_peers = [lax.rem(row + d, n_row) for d in range(1, n_row)]
    col_peers = [lax.rem(col + d, n_col) for d in range(1, n_col)]
    barrier = pltpu.get_barrier_semaphore()
    for peer in row_peers:
        pl.semaphore_signal(barrier, inc=1, device_id={"row": peer}, device_id_type=MESH)
    for peer in col_peers:
        pl.semaphore_signal(barrier, inc=1, device_id={"col": peer}, device_id_type=MESH)
    pl.semaphore_wait(barrier, n_row + n_col - 2)

    def gather_copy(step, peer, source):
        return pltpu.make_async_remote_copy(
            src_ref=newest.at[step],
            dst_ref=window.at[step, source],
            send_sem=ag_send.at[step, peer],
            recv_sem=ag_recv.at[step, source],
            device_id={"row": peer},
            device_id_type=MESH,
        )

    def start_gather(step, value):
        newest[step] = value
        for peer in row_peers:
            gather_copy(step, peer, row).start()
        window[step, row] = value

    def wait_gather(step):
        for peer in row_peers:
            gather_copy(step, peer, peer).wait_recv()

    def scatter_copy(step, peer, source):
        return pltpu.make_async_remote_copy(
            src_ref=force.at[step, peer],
            dst_ref=received.at[step, source],
            send_sem=rs_send.at[step, peer],
            recv_sem=rs_recv.at[step, source],
            device_id={"col": peer},
            device_id_type=MESH,
        )

    def exchange_copy(peer, source):
        return pltpu.make_async_remote_copy(
            src_ref=outgoing.at[peer],
            dst_ref=arrived.at[source],
            send_sem=ex_send.at[peer],
            recv_sem=ex_recv.at[source],
            device_id={"row": peer},
            device_id_type=MESH,
        )

    def lag_block(k, count=1):
        return kern[pl.ds(k, count)].reshape(count * depth, block)

    def window_of(step):
        return window[step].reshape(depth, reals)

    def history_force(step, group_size, wait):
        acc[...] = jnp.zeros_like(acc)
        for index, (first, last) in enumerate(wait):
            if step == 0:
                for copy in get_groups[index]:
                    copy.wait()
                for k in range(first - 1, last - 1):
                    hist_t[:, k * depth : (k + 1) * depth] = hist[k].reshape(depth, reals).T
            low, high = first - 1 - step, last - 1 - step
            acc[...] += dot(hist_t[:, low * depth : high * depth], lag_block(first, last - first))
        base_force[step] = acc[...].T

    get_v.wait()
    start_gather(0, v[...].astype(jnp.bfloat16))
    get_first.wait()
    k_t[0] = lag_block(0).T
    history_force(0, None, groups)

    def send_force(step):
        wait_gather(step)
        force[step] = (base_force[step] + dot(k_t[0], window_of(step))).reshape(n_col, slab, reals)
        for peer in col_peers:
            scatter_copy(step, peer, col).start()

    send_force(0)

    for copy in get_state:
        copy.wait()
    solve_wide = block_diagonal(solve, modules)
    stiff_wide = block_diagonal(stiff, modules)

    displacement, velocity, acceleration = x[...], v[...], a[...]
    for step in range(STEPS):
        predicted = displacement + DT * velocity + QUARTER * acceleration
        known = dot(solve_wide, exc[step] - dot(stiff_wide, predicted, EXACT), EXACT)
        drift = velocity + 0.5 * DT * (acceleration + known)
        if step == 0:
            for later in (1, 2):
                k_t[later] = lag_block(later).T
            history_force(1, None, [(k, min(k + 2, lags)) for k in range(2, lags, 2)])
            base_force[1] = base_force[1] + dot(k_t[1], window_of(0))
            base_force[2] = dot(k_t[2], window_of(0))
        if step == 1:
            first_part = base_force[2]
            history_force(2, None, [(k, min(k + 2, lags)) for k in range(3, lags, 2)])
            base_force[2] = base_force[2] + first_part + dot(k_t[1], window_of(1))
        if step == 2:
            for copy in get_tables:
                copy.wait()
            routing[...] = routing_matrix(owned[...], grid_index * modules, modules)
            gaps[...] = dot(
                gap_matrix(links, arms, grid_index * modules * POINTS, modules),
                choice_matrix(owned[...], row, col, n_col * modules, modules),
                EXACT,
            )
        for peer in col_peers:
            scatter_copy(step, peer, peer).wait_recv()
        received[step, col] = force[step, col]
        total = received[step, 0]
        for source in range(1, n_col):
            total = total + received[step, source]
        answer = dot(solve_wide, total, EXACT)
        velocity = drift - 0.5 * DT * answer
        if step + 1 < STEPS:
            start_gather(step + 1, velocity.astype(jnp.bfloat16))
        acceleration = known - answer
        displacement = predicted + QUARTER * acceleration
        if step + 1 < STEPS:
            send_force(step + 1)

    outgoing[...] = dot(routing[...], displacement, EXACT).reshape(n_row, LANE_ROWS, reals)
    for peer in row_peers:
        exchange_copy(peer, row).start()
    arrived[row] = outgoing[row]
    v_out[...] = velocity
    for step in range(STEPS):
        for peer in row_peers:
            gather_copy(step, peer, row).wait_send()
        for peer in col_peers:
            scatter_copy(step, peer, col).wait_send()
    for peer in row_peers:
        exchange_copy(peer, peer).wait_recv()
    deck_out[...] = dot(gaps[...], arrived[...].reshape(n_row * LANE_ROWS, reals), EXACT)
    for peer in row_peers:
        exchange_copy(peer, row).wait_send()


def body(
    n_row, n_col,
    kernel, history, displacement, velocity, acceleration, excitation, solve_inverse, stiffness, owned, links, arms,
):
    lags = kernel.shape[0]
    slab, reals = velocity.shape
    modules = slab // 6
    block = kernel.shape[3]
    depth = n_row * slab
    points = modules * POINTS * 3
    anywhere = pl.BlockSpec(memory_space=pl.ANY)
    in_vmem = pl.BlockSpec(memory_space=pltpu.VMEM)
    groups = [(k, min(k + 3, lags)) for k in range(1, lags, 3)]
    bf16, fp32, i32 = jnp.bfloat16, jnp.float32, jnp.int32
    vm = pltpu.VMEM
    owned = owned.reshape(n_row, n_col * modules)
    v_last, gaps = pl.pallas_call(
        functools.partial(steps_kernel, n_row, n_col, lags, groups),
        out_shape=(
            jax.ShapeDtypeStruct((slab, reals), fp32),
            jax.ShapeDtypeStruct((points, reals), fp32),
        ),
        in_specs=[anywhere] * 11,
        out_specs=(in_vmem, in_vmem),
        scratch_shapes=[
            vm(kernel.shape, bf16),
            vm(history.shape, bf16),
            vm((reals, (lags - 1) * depth), bf16),
            vm((slab, reals), fp32),
            vm((slab, reals), fp32),
            vm((slab, reals), fp32),
            vm(excitation.shape, fp32),
            vm(solve_inverse.shape, fp32),
            vm(stiffness.shape, fp32),
            vm(owned.shape, i32),
            vm(links.shape, i32),
            vm(arms.shape, fp32),
            vm((3, block, depth), bf16),
            vm((reals, block), fp32),
            vm((STEPS, block, reals), fp32),
            vm((STEPS, n_col, slab, reals), fp32),
            vm((STEPS, slab, reals), bf16),
            vm((STEPS, n_row, slab, reals), bf16),
            vm((STEPS, n_col, slab, reals), fp32),
            vm((n_row, LANE_ROWS, reals), fp32),
            vm((n_row, LANE_ROWS, reals), fp32),
            vm((points, n_row * LANE_ROWS), fp32),
            vm((n_row * LANE_ROWS, slab), fp32),
            pltpu.SemaphoreType.DMA((32,)),
            pltpu.SemaphoreType.DMA((STEPS, n_row)),
            pltpu.SemaphoreType.DMA((STEPS, n_row)),
            pltpu.SemaphoreType.DMA((STEPS, n_col)),
            pltpu.SemaphoreType.DMA((STEPS, n_col)),
            pltpu.SemaphoreType.DMA((n_row,)),
            pltpu.SemaphoreType.DMA((n_row,)),
        ],
        compiler_params=pltpu.CompilerParams(
            collective_id=0, has_side_effects=True, vmem_limit_bytes=56 * 1024 * 1024
        ),
    )(kernel, history, displacement, velocity, acceleration, excitation, solve_inverse, stiffness, owned, links, arms)
    return v_last, gaps.reshape(modules, POINTS, 3, reals)


def solution(mesh):
    placed = (
        P(None, None, "col", "row"),
        P(None, None, "col", "sea"),
        P(("row", "col"), "sea"),
        P(("row", "col"), "sea"),
        P(("row", "col"), "sea"),
        P(None, ("row", "col"), "sea"),
        P(("row", "col"), None, None),
        P(("row", "col"), None, None),
        P(),
        P(("row", "col"), None),
        P(("row", "col"), None, None),
    )
    return jax.shard_map(
        functools.partial(body, mesh.shape["row"], mesh.shape["col"]),
        mesh=mesh,
        in_specs=placed,
        out_specs=(P(("row", "col"), "sea"), P(("row", "col"), None, None, "sea")),
        check_vma=False,
    )
```

time: 379 us -> 99.2 us (0.26)
  the two profiles are of different devices: /device:TPU:2 before, /device:TPU:64 now
where the time goes in v1:
time: 99.2 us; the launch traced here: 98.9 us
  Pallas kernels  90.8 us (92%)
  local copies, waits for them, and re-layouts  7.43 us (7%)
    pallas_call x1, Pallas kernels, body(): pl.pallas_call(functools.partial(steps_kernel, n_row, n_col, lags, groups...  90.8 us
    unnamed x5, local copies, waits for them, and re-layouts  6.27 us

profile of v1, /device:TPU:64, one launch (start us, length us, event | category | flops | bytes accessed | tf_op | source)
XLA Modules:
  0.0 98.9 jit_solution(11955105476413805258)
XLA Ops:
  0.6 1.3 %copy.19.arms_hbm = f32[8,3,16]{2,1,0:T(4,128)} copy(f32[8,3,16]{2,0,1:T(8,128)} %param.21) | data formatting | bytes 3072 | tf_op args[10]
  1.9 1.4 %copy.17.solve_hbm = f32[8,6,6]{2,1,0:T(8,128)} copy(f32[8,6,6]{2,0,1:T(8,128)} %param.17) | data formatting | bytes 2304 | tf_op args[6]
  3.3 1.4 %copy.18.stiff_hbm = f32[8,6,6]{2,1,0:T(8,128)} copy(f32[8,6,6]{2,0,1:T(8,128)} %param.18) | data formatting | bytes 2304 | tf_op args[7]
  4.7 90.8 %shard_map.122 = (f32[48,256]{1,0:T(8,128)}, f32[384,256]{1,0:T(8,128)}) custom-call(bf16[16,8,48,768]{3,2,1,0:T(8,128)(2,1)} %kernel_hbm.1, bf16[15,8,48,256]{3,2,1,0:T(8,128)(2,1)} %history_hbm.1, f32[48,256]{1,0:T(8,128)} %x_hbm.1, f32[48,256]{1,0:T(8,128)} %v_hbm.1, f32[48,256]{1,0:T(8,128)} %a_hbm.1, f32[3,48,256]{2,1,0:T(8,128)} %exc_hbm.1, ...), custom_call_target="tpu_custom_call" | custom-call | tf_op jit(solution)/shard_map/pallas_call | solution.py:313
  95.5 1.2 %reshape.11 = f32[8,16,3,256]{3,2,1,0:T(4,128)S(1)} reshape(f32[384,256]{1,0:T(8,128)} %get-tuple-element.5) | data formatting | bytes 786432 | tf_op jit(solution)/shard_map/reshape | solution.py:357
  96.6 0.8 copy.20
  97.4 1.4 %copy.22 = f32[48,256]{1,0:T(8,128)} copy(f32[48,256]{1,0:T(8,128)} %get-tuple-element.12) | data formatting | bytes 98304

commit v2 on v1

v2 whole, which is shorter than its diff:
```python
import functools

import jax
import jax.numpy as jnp
from jax import lax
from jax.experimental import pallas as pl
from jax.experimental.pallas import tpu as pltpu
from jax.sharding import PartitionSpec as P

POINTS = 16
STEPS = 3
SLOTS = 2
LANE_ROWS = 16

DT = 0.5
QUARTER = DT * DT / 4.0
TOP = 32000.0
PAIR = 2
MESH = pl.DeviceIdType.MESH
EXACT = lax.Precision.HIGHEST


def iota(shape, dim):
    return lax.broadcasted_iota(jnp.int32, shape, dim)


def f32(mask):
    return jnp.where(mask, 1.0, 0.0).astype(jnp.float32)


def dot(a, b, precision=None):
    return lax.dot_general(
        a, b, (((1,), (0,)), ((), ())), precision=precision, preferred_element_type=jnp.float32
    )


def dot_nt(a, b, precision=None):
    return lax.dot_general(
        a, b, (((1,), (1,)), ((), ())), precision=precision, preferred_element_type=jnp.float32
    )


def pieces(value, count):
    out = []
    for _ in range(count):
        out.append(value.astype(jnp.bfloat16))
        value = value - out[-1].astype(jnp.float32)
    return out


def left_pieces(matrix):
    high, low = pieces(matrix, 2)
    return jnp.concatenate([high, high, low, low], axis=1)


def right_pieces(matrix):
    high, low = pieces(matrix, 2)
    return jnp.concatenate([high, low, high, low], axis=0)


def block_diagonal(ref, modules):
    size = 6 * modules
    column = iota((size, size), 1)
    repeat = f32(iota((6, size), 1) % 6 == iota((6, size), 0))
    by_row = dot(ref[...].reshape(size, 6), repeat, EXACT)
    by_row = jnp.where(column // 6 == iota((size, size), 0) % modules, by_row, 0.0)
    order = f32(column == iota((size, size), 0) % 6 * modules + iota((size, size), 0) // 6)
    return dot(order, by_row, EXACT)


def routing_matrix(owned, base, modules):
    n_row, lanes = owned.shape
    lane = iota((n_row, lanes), 1)
    column = iota((n_row, modules), 1)
    out_rows = n_row * LANE_ROWS
    spread = f32(iota((modules, 6 * modules), 1) // 6 == iota((modules, 6 * modules), 0))
    total = jnp.zeros((out_rows, 6 * modules), jnp.float32)
    for slot in range(SLOTS):
        hit = jnp.zeros((n_row, modules), jnp.float32)
        for m in range(modules):
            here = f32((owned == base + m) & (lane % SLOTS == slot))
            hit = jnp.where(column == m, jnp.sum(here, axis=1, keepdims=True), hit)
        r = iota((out_rows, n_row), 0)
        lift = f32(
            (r // LANE_ROWS == iota((out_rows, n_row), 1))
            & (r % LANE_ROWS >= 6 * slot)
            & (r % LANE_ROWS < 6 * slot + 6)
        )
        wide = dot(dot(lift, hit), spread)
        rr = iota((out_rows, 6 * modules), 0) % LANE_ROWS - 6 * slot
        total = total + jnp.where(rr == iota((out_rows, 6 * modules), 1) % 6, wide, 0.0)
    return total


def choice_matrix(owned, row, col, home_size, modules):
    n_row, lanes = owned.shape
    home = owned // home_size
    mine = jnp.sum(jnp.where(iota((n_row, lanes), 0) == row, home, 0), axis=0, keepdims=True)
    per_lane = f32(iota((n_row, lanes), 0) == mine)
    size = 6 * modules
    pick = f32(iota((size, lanes), 1) == col * modules + iota((size, lanes), 0) // 6)
    by_row = dot_nt(pick, per_lane)
    out = n_row * LANE_ROWS
    widen = f32(iota((n_row, out), 1) // LANE_ROWS == iota((n_row, out), 0))
    wide = dot(by_row, widen)
    i = iota((size, out), 0)
    fits = iota((size, out), 1) % LANE_ROWS == 6 * (i // 6 % SLOTS) + i % 6
    return jnp.where(fits, wide, 0.0)


def gap_matrix(links_ref, arms_ref, first_point, modules):
    rows, size = 3 * POINTS, 6 * modules
    by_point = f32(iota((rows, POINTS), 0) % POINTS == iota((rows, POINTS), 1))
    levers = dot_nt(by_point, arms_ref[...].reshape(3 * modules, POINTS), EXACT)
    lane = iota((rows, size), 1)
    comp = iota((rows, size), 0) // POINTS
    mode = lane % 6
    spread = f32(iota((modules, size), 1) // 6 == iota((modules, size), 0))
    form = f32(mode == comp)
    for d in range(3):
        along = dot(levers[:, d * modules : (d + 1) * modules], spread, EXACT)
        form = form + jnp.where((mode == 3 + (comp + 1) % 3) & ((comp + 2) % 3 == d), along, 0.0)
        form = form - jnp.where((mode == 3 + (comp + 2) % 3) & ((comp + 1) % 3 == d), along, 0.0)
    local = (links_ref[...] - first_point).astype(jnp.float32)
    partner = dot_nt(by_point, local, EXACT).astype(jnp.int32)
    wide = iota((rows, rows), 1)
    same = wide // POINTS == iota((rows, rows), 0) // POINTS
    picks = [f32((partner[:, t : t + 1] % POINTS == wide % POINTS) & same) for t in range(modules)]
    other = dot(jnp.concatenate(picks, axis=0), form, EXACT)
    out = []
    for t in range(modules):
        theirs = other[t * rows : (t + 1) * rows]
        out.append(
            jnp.where(lane // 6 == t, form, 0.0)
            - jnp.where(lane // 6 == partner[:, t : t + 1] // POINTS, theirs, 0.0)
        )
    return jnp.concatenate(out, axis=0)


def coded(value, top):
    scale = jnp.where(top > 1e-30, TOP / jnp.maximum(top, 1e-30), 0.0)
    return jnp.round(value * scale).astype(jnp.int32).astype(jnp.int16)


def decoded(code, top):
    return code.astype(jnp.int32).astype(jnp.float32) * (top * (1.0 / TOP))


def largest(value):
    flat = value.reshape(-1, value.shape[-1])
    return jnp.max(jnp.abs(flat), axis=0, keepdims=True)


def steps_kernel(
    n_row, n_col, lags, groups,
    kernel_hbm, history_hbm, x_hbm, v_hbm, a_hbm, exc_hbm, solve_hbm, stiff_hbm, owned_hbm, links_hbm, arms_hbm,
    v_out, deck_out,
    kern, hist, past_t, x, v, a, exc, solve, stiff, owned, links, arms,
    k_t, acc, base_force, own_force, newest, window, pair_out, pair_in, line_out, line_in, outgoing, arrived,
    gaps, routing, pair_top_out, pair_top_in, line_top_out, line_top_in,
    local_sem, ag_send, ag_recv, pair_send, pair_recv, line_send, line_recv, top_send, top_recv, ex_send, ex_recv,
):
    row, col = lax.axis_index("row"), lax.axis_index("col")
    slab, reals = v.shape
    modules = slab // 6
    depth = n_row * slab
    block = n_col * slab
    half = block // PAIR
    n_line = n_col // PAIR
    grid_index = row * n_col + col
    line, side = col // PAIR, lax.rem(col, PAIR)
    other = 1 - side
    partner = line * PAIR + other

    sems = iter(range(64))

    def fetch(src, dst):
        copy = pltpu.make_async_copy(src, dst, local_sem.at[next(sems)])
        copy.start()
        return copy

    get_v = fetch(v_hbm, v)
    get_first = fetch(kernel_hbm.at[pl.ds(0, 1)], kern.at[pl.ds(0, 1)])
    get_groups = []
    for first, last in groups:
        get_groups.append(
            (
                fetch(history_hbm.at[pl.ds(first - 1, last - first)], hist.at[pl.ds(first - 1, last - first)]),
                fetch(kernel_hbm.at[pl.ds(first, last - first)], kern.at[pl.ds(first, last - first)]),
            )
        )
    get_state = [fetch(x_hbm, x), fetch(a_hbm, a), fetch(exc_hbm, exc), fetch(solve_hbm, solve), fetch(stiff_hbm, stiff)]
    get_tables = [fetch(owned_hbm, owned), fetch(links_hbm, links), fetch(arms_hbm, arms)]

    row_peers = [lax.rem(row + d, n_row) for d in range(1, n_row)]
    far_first = sorted(range(1, n_line), key=lambda d: -min(d, n_line - d))
    line_peers = [lax.rem(line + d, n_line) for d in far_first]

    barrier = pltpu.get_barrier_semaphore()
    for peer in row_peers:
        pl.semaphore_signal(barrier, inc=1, device_id={"row": peer}, device_id_type=MESH)
    pl.semaphore_signal(barrier, inc=1, device_id={"col": partner}, device_id_type=MESH)
    for peer in line_peers:
        pl.semaphore_signal(barrier, inc=1, device_id={"col": peer * PAIR + side}, device_id_type=MESH)
    pl.semaphore_wait(barrier, n_row - 1 + 1 + n_line - 1)

    def gather_copy(step, peer, source):
        return pltpu.make_async_remote_copy(
            src_ref=newest.at[step],
            dst_ref=window.at[step, source],
            send_sem=ag_send.at[step, peer],
            recv_sem=ag_recv.at[step, source],
            device_id={"row": peer},
            device_id_type=MESH,
        )

    def start_gather(step, value):
        newest[step] = value
        for peer in row_peers:
            gather_copy(step, peer, row).start()
        window[step, row] = value

    def wait_gather(step):
        for peer in row_peers:
            gather_copy(step, peer, peer).wait_recv()

    def pair_copy(step, piece):
        return pltpu.make_async_remote_copy(
            src_ref=pair_out.at[step, piece],
            dst_ref=pair_in.at[step, piece],
            send_sem=pair_send.at[step, piece],
            recv_sem=pair_recv.at[step, piece],
            device_id={"col": partner},
            device_id_type=MESH,
        )

    def pair_top_copy(step):
        return pltpu.make_async_remote_copy(
            src_ref=pair_top_out.at[step],
            dst_ref=pair_top_in.at[step],
            send_sem=top_send.at[step, n_line],
            recv_sem=top_recv.at[step, n_line],
            device_id={"col": partner},
            device_id_type=MESH,
        )

    def line_copy(step, peer, source):
        return pltpu.make_async_remote_copy(
            src_ref=line_out.at[step, peer],
            dst_ref=line_in.at[step, source],
            send_sem=line_send.at[step, peer],
            recv_sem=line_recv.at[step, source],
            device_id={"col": peer * PAIR + side},
            device_id_type=MESH,
        )

    def line_top_copy(step, peer, source):
        return pltpu.make_async_remote_copy(
            src_ref=line_top_out.at[step],
            dst_ref=line_top_in.at[step, source],
            send_sem=top_send.at[step, peer],
            recv_sem=top_recv.at[step, source],
            device_id={"col": peer * PAIR + side},
            device_id_type=MESH,
        )

    def exchange_copy(peer, source):
        return pltpu.make_async_remote_copy(
            src_ref=outgoing.at[peer],
            dst_ref=arrived.at[source],
            send_sem=ex_send.at[peer],
            recv_sem=ex_recv.at[source],
            device_id={"row": peer},
            device_id_type=MESH,
        )

    def window_of(step):
        return window[step].reshape(depth, reals)

    def lag_share(step, first, last):
        low = (first + 1 - step) * depth
        high = (last + 1 - step) * depth
        lag_block = kern[first:last].reshape((last - first) * depth, block)
        return dot(past_t[:, low:high], lag_block)

    def add_lags(step, index, fresh):
        share = lag_share(step, *groups[index])
        if fresh:
            acc[...] = share
        else:
            acc[...] += share

    def close_lags(step):
        base_force[step] = acc[...].T.reshape(n_line, PAIR, slab, reals)

    get_v.wait()
    start_gather(0, v[...].astype(jnp.bfloat16))
    get_first.wait()
    k_t[...] = kern[0].reshape(depth, block).T.reshape(n_line, PAIR, slab, depth)
    for index, (first, last) in enumerate(groups):
        for copy in get_groups[index]:
            copy.wait()
        for k in range(first - 1, last - 1):
            past_t[:, (k + 2) * depth : (k + 3) * depth] = hist[k].reshape(depth, reals).T
        add_lags(0, index, index == 0)
    close_lags(0)

    def half_force(step, which):
        now = dot(k_t[:, which].reshape(half, depth), window_of(step))
        return base_force[step, :, which] + now.reshape(n_line, slab, reals)

    def send_force(step):
        wait_gather(step)
        theirs = half_force(step, other)
        top = largest(theirs)
        pair_top_out[step] = top
        pair_top_copy(step).start()
        own_force[...] = theirs
        for piece in [*line_peers, line]:
            pair_out[step, piece] = coded(own_force[piece], top)
            pair_copy(step, piece).start()
        mine = half_force(step, side)
        own_force[...] = mine
        return largest(mine)

    def pass_on(step, own_top, fillers):
        fillers = list(fillers)
        pair_top_copy(step).wait_recv()
        top_in = pair_top_in[step]
        top = own_top + top_in
        line_top_out[step] = top
        for peer in line_peers:
            line_top_copy(step, peer, line).start()
        for peer in line_peers:
            pair_copy(step, peer).wait_recv()
            line_out[step, peer] = coded(own_force[peer] + decoded(pair_in[step, peer], top_in), top)
            line_copy(step, peer, line).start()
            if fillers:
                fillers.pop(0)()
        pair_copy(step, line).wait_recv()
        total = own_force[line] + decoded(pair_in[step, line], top_in)
        own_force[line] = total
        for filler in fillers:
            filler()
        total = own_force[line]
        for peer in line_peers:
            line_top_copy(step, peer, peer).wait_recv()
            line_copy(step, peer, peer).wait_recv()
            total = total + decoded(line_in[step, peer], line_top_in[step, peer])
        return total

    own_top = send_force(0)

    for copy in get_state:
        copy.wait()
    solve_left = left_pieces(block_diagonal(solve, modules))
    stiff_left = left_pieces(block_diagonal(stiff, modules))

    def newest_past(step):
        past_t[:, (1 - step) * depth : (2 - step) * depth] = window_of(step).T

    def fill_lags(step):
        order = [*range(1, len(groups)), 0]
        return [functools.partial(add_lags, step, index, i == 0) for i, index in enumerate(order)] + [
            functools.partial(close_lags, step)
        ]

    def tables():
        for copy in get_tables:
            copy.wait()
        route = routing_matrix(owned[...], grid_index * modules, modules).astype(jnp.bfloat16)
        routing[...] = jnp.concatenate([route, route, route], axis=1)
        forms = dot(
            gap_matrix(links, arms, grid_index * modules * POINTS, modules),
            choice_matrix(owned[...], row, col, n_col * modules, modules),
            EXACT,
        )
        gaps[...] = left_pieces(forms)

    displacement, velocity, acceleration = x[...], v[...], a[...]
    for step in range(STEPS):
        predicted = displacement + DT * velocity + QUARTER * acceleration
        known = dot(solve_left, right_pieces(exc[step] - dot(stiff_left, right_pieces(predicted))))
        drift = velocity + 0.5 * DT * (acceleration + known)
        if step + 1 < STEPS:
            newest_past(step)
        total = pass_on(step, own_top, fill_lags(step + 1) if step + 1 < STEPS else [tables])
        answer = dot(solve_left, right_pieces(total))
        velocity = drift - 0.5 * DT * answer
        if step + 1 < STEPS:
            start_gather(step + 1, velocity.astype(jnp.bfloat16))
        acceleration = known - answer
        displacement = predicted + QUARTER * acceleration
        if step + 1 < STEPS:
            own_top = send_force(step + 1)

    leaving = dot(routing[...], jnp.concatenate(pieces(displacement, 3), axis=0))
    outgoing[...] = leaving.reshape(n_row, LANE_ROWS, reals)
    for peer in row_peers:
        exchange_copy(peer, row).start()
    arrived[row] = outgoing[row]
    v_out[...] = velocity
    for step in range(STEPS):
        for peer in row_peers:
            gather_copy(step, peer, row).wait_send()
        pair_top_copy(step).wait_send()
        for piece in [*line_peers, line]:
            pair_copy(step, piece).wait_send()
        for peer in line_peers:
            line_top_copy(step, peer, line).wait_send()
            line_copy(step, peer, line).wait_send()
    for peer in row_peers:
        exchange_copy(peer, peer).wait_recv()
    deck_out[...] = dot(gaps[...], right_pieces(arrived[...].reshape(n_row * LANE_ROWS, reals)))
    for peer in row_peers:
        exchange_copy(peer, row).wait_send()


def body(
    n_row, n_col,
    kernel, history, displacement, velocity, acceleration, excitation, solve_inverse, stiffness, owned, links, arms,
):
    lags = kernel.shape[0]
    slab, reals = velocity.shape
    modules = slab // 6
    block = kernel.shape[3]
    depth = n_row * slab
    n_line = n_col // PAIR
    points = modules * POINTS * 3
    arrivals = n_row * LANE_ROWS
    anywhere = pl.BlockSpec(memory_space=pl.ANY)
    in_vmem = pl.BlockSpec(memory_space=pltpu.VMEM)
    groups = [(1, 2)] + [(k, min(k + 2, lags)) for k in range(2, lags, 2)]
    bf16, fp32, i32, i16 = jnp.bfloat16, jnp.float32, jnp.int32, jnp.int16
    vm = pltpu.VMEM
    sems = pltpu.SemaphoreType.DMA
    owned = owned.reshape(n_row, n_col * modules)
    solve_inverse = solve_inverse.transpose(1, 0, 2)
    stiffness = stiffness.transpose(1, 0, 2)
    arms = arms.transpose(1, 0, 2)
    v_last, gaps = pl.pallas_call(
        functools.partial(steps_kernel, n_row, n_col, lags, groups),
        out_shape=(
            jax.ShapeDtypeStruct((slab, reals), fp32),
            jax.ShapeDtypeStruct((points, reals), fp32),
        ),
        in_specs=[anywhere] * 11,
        out_specs=(in_vmem, in_vmem),
        scratch_shapes=[
            vm(kernel.shape, bf16),
            vm(history.shape, bf16),
            vm((reals, (lags + 1) * depth), bf16),
            vm((slab, reals), fp32),
            vm((slab, reals), fp32),
            vm((slab, reals), fp32),
            vm(excitation.shape, fp32),
            vm(solve_inverse.shape, fp32),
            vm(stiffness.shape, fp32),
            vm(owned.shape, i32),
            vm(links.shape, i32),
            vm(arms.shape, fp32),
            vm((n_line, PAIR, slab, depth), bf16),
            vm((reals, block), fp32),
            vm((STEPS, n_line, PAIR, slab, reals), fp32),
            vm((n_line, slab, reals), fp32),
            vm((STEPS, slab, reals), bf16),
            vm((STEPS, n_row, slab, reals), bf16),
            vm((STEPS, n_line, slab, reals), i16),
            vm((STEPS, n_line, slab, reals), i16),
            vm((STEPS, n_line, slab, reals), i16),
            vm((STEPS, n_line, slab, reals), i16),
            vm((n_row, LANE_ROWS, reals), fp32),
            vm((n_row, LANE_ROWS, reals), fp32),
            vm((points, 4 * arrivals), bf16),
            vm((arrivals, 3 * slab), bf16),
            vm((STEPS, 1, reals), fp32),
            vm((STEPS, 1, reals), fp32),
            vm((STEPS, 1, reals), fp32),
            vm((STEPS, n_line, 1, reals), fp32),
            sems((32,)),
            sems((STEPS, n_row)),
            sems((STEPS, n_row)),
            sems((STEPS, n_line)),
            sems((STEPS, n_line)),
            sems((STEPS, n_line)),
            sems((STEPS, n_line)),
            sems((STEPS, n_line + 1)),
            sems((STEPS, n_line + 1)),
            sems((n_row,)),
            sems((n_row,)),
        ],
        compiler_params=pltpu.CompilerParams(
            collective_id=0, has_side_effects=True, vmem_limit_bytes=56 * 1024 * 1024
        ),
    )(kernel, history, displacement, velocity, acceleration, excitation, solve_inverse, stiffness, owned, links, arms)
    return v_last, gaps.reshape(modules, 3, POINTS, reals).transpose(0, 2, 1, 3)


def solution(mesh):
    placed = (
        P(None, None, "col", "row"),
        P(None, None, "col", "sea"),
        P(("row", "col"), "sea"),
        P(("row", "col"), "sea"),
        P(("row", "col"), "sea"),
        P(None, ("row", "col"), "sea"),
        P(("row", "col"), None, None),
        P(("row", "col"), None, None),
        P(),
        P(("row", "col"), None),
        P(("row", "col"), None, None),
    )
    return jax.shard_map(
        functools.partial(body, mesh.shape["row"], mesh.shape["col"]),
        mesh=mesh,
        in_specs=placed,
        out_specs=(P(("row", "col"), "sea"), P(("row", "col"), None, None, "sea")),
        check_vma=False,
    )
```

time: 99.2 us -> 70 us (0.71)
  the two profiles are of different devices: /device:TPU:64 before, /device:TPU:2 now
where the time goes in v2:
time: 70 us; the launch traced here: 69 us
  Pallas kernels  65.2 us (93%)
  local copies, waits for them, and re-layouts  3.19 us (5%)
    pallas_call x1, Pallas kernels, body(): pl.pallas_call(functools.partial(steps_kernel, n_row, n_col, lags, groups...  65.2 us
    unnamed x2, local copies, waits for them, and re-layouts  3.19 us

profile of v2, /device:TPU:2, one launch (start us, length us, event | category | flops | bytes accessed | tf_op | source)
XLA Modules:
  0.0 69.0 jit_solution(1670582548344794426)
XLA Ops:
  0.6 65.2 %shard_map.122 = (f32[48,256]{1,0:T(8,128)}, f32[384,256]{1,0:T(8,128)}) custom-call(bf16[16,8,48,768]{3,2,1,0:T(8,128)(2,1)} %kernel_hbm.1, bf16[15,8,48,256]{3,2,1,0:T(8,128)(2,1)} %history_hbm.1, f32[48,256]{1,0:T(8,128)} %x_hbm.1, f32[48,256]{1,0:T(8,128)} %v_hbm.1, f32[48,256]{1,0:T(8,128)} %a_hbm.1, f32[3,48,256]{2,1,0:T(8,128)} %exc_hbm.1, ...), custom_call_target="tpu_custom_call" | custom-call | tf_op jit(solution)/shard_map/pallas_call | solution.py:441
  65.8 1.4 %copy.15 = f32[48,256]{1,0:T(8,128)} copy(f32[48,256]{1,0:T(8,128)} %get-tuple-element.8) | data formatting | bytes 98304
  67.2 1.8 %copy.16 = f32[8,16,3,256]{3,1,2,0:T(8,128)} copy(f32[8,16,3,256]{3,1,2,0:T(8,128)} %bitcast.7) | data formatting | bytes 786432

commit v3 on v2

--- a/solution.py
+++ b/solution.py
@@ -16,6 +16,7 @@
 QUARTER = DT * DT / 4.0
 TOP = 32000.0
 PAIR = 2
+ROW_RING = 4
 MESH = pl.DeviceIdType.MESH
 EXACT = lax.Precision.HIGHEST
 
@@ -192,7 +193,13 @@
     get_state = [fetch(x_hbm, x), fetch(a_hbm, a), fetch(exc_hbm, exc), fetch(solve_hbm, solve), fetch(stiff_hbm, stiff)]
     get_tables = [fetch(owned_hbm, owned), fetch(links_hbm, links), fetch(arms_hbm, arms)]
 
-    row_peers = [lax.rem(row + d, n_row) for d in range(1, n_row)]
+    ring, turn = row % ROW_RING, row // ROW_RING
+    row_peers = [
+        lax.rem(turn + t, n_row // ROW_RING) * ROW_RING + lax.rem(ring + d, ROW_RING)
+        for t in (1, 0)
+        for d in (2, 1, 3, 0)
+        if t or d
+    ]
     far_first = sorted(range(1, n_line), key=lambda d: -min(d, n_line - d))
     line_peers = [lax.rem(line + d, n_line) for d in far_first]
 
@@ -323,8 +330,9 @@
         own_force[...] = mine
         return largest(mine)
 
-    def pass_on(step, own_top, fillers):
-        fillers = list(fillers)
+    def pass_on(step, own_top, early, late):
+        for filler in early:
+            filler()
         pair_top_copy(step).wait_recv()
         top_in = pair_top_in[step]
         top = own_top + top_in
@@ -335,12 +343,10 @@
             pair_copy(step, peer).wait_recv()
             line_out[step, peer] = coded(own_force[peer] + decoded(pair_in[step, peer], top_in), top)
             line_copy(step, peer, line).start()
-            if fillers:
-                fillers.pop(0)()
         pair_copy(step, line).wait_recv()
         total = own_force[line] + decoded(pair_in[step, line], top_in)
         own_force[line] = total
-        for filler in fillers:
+        for filler in late:
             filler()
         total = own_force[line]
         for peer in line_peers:
@@ -358,12 +364,6 @@
 
     def newest_past(step):
         past_t[:, (1 - step) * depth : (2 - step) * depth] = window_of(step).T
-
-    def fill_lags(step):
-        order = [*range(1, len(groups)), 0]
-        return [functools.partial(add_lags, step, index, i == 0) for i, index in enumerate(order)] + [
-            functools.partial(close_lags, step)
-        ]
 
     def tables():
         for copy in get_tables:
@@ -377,6 +377,16 @@
         )
         gaps[...] = left_pieces(forms)
 
+    def fill_lags(step):
+        order = [*range(1, len(groups)), 0]
+        return [functools.partial(add_lags, step, index, i == 0) for i, index in enumerate(order)] + [
+            functools.partial(close_lags, step)
+        ]
+
+    fillers = [fill_lags(1), fill_lags(2), [tables]]
+    early_ends, late_ends = (0, 1, 0), (3, 4, 1)
+
+
     displacement, velocity, acceleration = x[...], v[...], a[...]
     for step in range(STEPS):
         predicted = displacement + DT * velocity + QUARTER * acceleration
@@ -384,13 +394,16 @@
         drift = velocity + 0.5 * DT * (acceleration + known)
         if step + 1 < STEPS:
             newest_past(step)
-        total = pass_on(step, own_top, fill_lags(step + 1) if step + 1 < STEPS else [tables])
+        work = fillers[step]
+        total = pass_on(step, own_top, work[: early_ends[step]], work[early_ends[step] : late_ends[step]])
         answer = dot(solve_left, right_pieces(total))
         velocity = drift - 0.5 * DT * answer
         if step + 1 < STEPS:
             start_gather(step + 1, velocity.astype(jnp.bfloat16))
         acceleration = known - answer
         displacement = predicted + QUARTER * acceleration
+        for filler in work[late_ends[step] :]:
+            filler()
         if step + 1 < STEPS:
             own_top = send_force(step + 1)
 
@@ -430,7 +443,7 @@
     arrivals = n_row * LANE_ROWS
     anywhere = pl.BlockSpec(memory_space=pl.ANY)
     in_vmem = pl.BlockSpec(memory_space=pltpu.VMEM)
-    groups = [(1, 2)] + [(k, min(k + 2, lags)) for k in range(2, lags, 2)]
+    groups = [(1, 2)] + [(k, min(k + 4, lags)) for k in range(2, lags, 4)]
     bf16, fp32, i32, i16 = jnp.bfloat16, jnp.float32, jnp.int32, jnp.int16
     vm = pltpu.VMEM
     sems = pltpu.SemaphoreType.DMA
@@ -440,10 +453,7 @@
     arms = arms.transpose(1, 0, 2)
     v_last, gaps = pl.pallas_call(
         functools.partial(steps_kernel, n_row, n_col, lags, groups),
-        out_shape=(
-            jax.ShapeDtypeStruct((slab, reals), fp32),
-            jax.ShapeDtypeStruct((points, reals), fp32),
-        ),
+        out_shape=(vm((slab, reals), fp32), vm((points, reals), fp32)),
         in_specs=[anywhere] * 11,
         out_specs=(in_vmem, in_vmem),
         scratch_shapes=[

time: 70 us -> 62.3 us (0.89); the launches traced: 69 us -> 62.2 us
  Pallas kernels: 65.2 us -> 60.2 us
  local copies, waits for them, and re-layouts: 3.19 us -> 1.37 us
    pallas_call x1, Pallas kernels: 65.2 us -> 60.2 us  [body(): pl.pallas_call(functools.partial(steps_kernel, n_row, n_col, lags, groups...]
    unnamed x2, local copies, waits for them, and re-layouts: 3.19 us -> 1.37 us
where the time goes in v3:
time: 62.3 us; the launch traced here: 62.2 us
  Pallas kernels  60.2 us (97%)
  local copies, waits for them, and re-layouts  1.37 us (2%)
  between operations  0.64 us (1%)
    pallas_call x1, Pallas kernels, body(): pl.pallas_call(functools.partial(steps_kernel, n_row, n_col, lags, groups...  60.2 us
    unnamed x2, local copies, waits for them, and re-layouts  1.37 us

profile of v3, /device:TPU:2, one launch (start us, length us, event | category | flops | bytes accessed | tf_op | source)
XLA Modules:
  0.0 62.2 jit_solution(3994705140928071530)
XLA Ops:
  0.6 60.2 %shard_map.122 = (f32[48,256]{1,0:T(8,128)S(1)}, f32[384,256]{1,0:T(8,128)S(1)}) custom-call(bf16[16,8,48,768]{3,2,1,0:T(8,128)(2,1)} %kernel_hbm.1, bf16[15,8,48,256]{3,2,1,0:T(8,128)(2,1)} %history_hbm.1, f32[48,256]{1,0:T(8,128)} %x_hbm.1, f32[48,256]{1,0:T(8,128)} %v_hbm.1, f32[48,256]{1,0:T(8,128)} %a_hbm.1, f32[3,48,256]{2,1,0:T(8,128)} %exc_hbm.1, ...), custom_call_target="tpu_custom_call" | custom-call | tf_op jit(solution)/shard_map/pallas_call | solution.py:454
  60.8 0.6 %copy.15 = f32[48,256]{1,0:T(8,128)} copy(f32[48,256]{1,0:T(8,128)S(1)} %get-tuple-element.6) | data formatting | bytes 98304
  61.5 0.7 %copy.16 = f32[8,16,3,256]{3,1,2,0:T(8,128)} copy(f32[8,16,3,256]{3,1,2,0:T(8,128)S(1)} %bitcast.7) | data formatting | bytes 786432

commit v4 on v3

--- a/solution.py
+++ b/solution.py
@@ -17,6 +17,7 @@
 TOP = 32000.0
 PAIR = 2
 ROW_RING = 4
+PARTS = 2
 MESH = pl.DeviceIdType.MESH
 EXACT = lax.Precision.HIGHEST
 
@@ -158,7 +159,7 @@
     v_out, deck_out,
     kern, hist, past_t, x, v, a, exc, solve, stiff, owned, links, arms,
     k_t, acc, base_force, own_force, newest, window, pair_out, pair_in, line_out, line_in, outgoing, arrived,
-    gaps, routing, pair_top_out, pair_top_in, line_top_out, line_top_in,
+    gaps, weights, base_out, predicted_last, pair_top_out, pair_top_in, line_top_out, line_top_in,
     local_sem, ag_send, ag_recv, pair_send, pair_recv, line_send, line_recv, top_send, top_recv, ex_send, ex_recv,
 ):
     row, col = lax.axis_index("row"), lax.axis_index("col")
@@ -167,6 +168,7 @@
     depth = n_row * slab
     block = n_col * slab
     half = block // PAIR
+    wide = reals // PARTS
     n_line = n_col // PAIR
     grid_index = row * n_col + col
     line, side = col // PAIR, lax.rem(col, PAIR)
@@ -190,9 +192,6 @@
                 fetch(kernel_hbm.at[pl.ds(first, last - first)], kern.at[pl.ds(first, last - first)]),
             )
         )
-    get_state = [fetch(x_hbm, x), fetch(a_hbm, a), fetch(exc_hbm, exc), fetch(solve_hbm, solve), fetch(stiff_hbm, stiff)]
-    get_tables = [fetch(owned_hbm, owned), fetch(links_hbm, links), fetch(arms_hbm, arms)]
-
     ring, turn = row % ROW_RING, row // ROW_RING
     row_peers = [
         lax.rem(turn + t, n_row // ROW_RING) * ROW_RING + lax.rem(ring + d, ROW_RING)
@@ -211,78 +210,80 @@
         pl.semaphore_signal(barrier, inc=1, device_id={"col": peer * PAIR + side}, device_id_type=MESH)
     pl.semaphore_wait(barrier, n_row - 1 + 1 + n_line - 1)
 
-    def gather_copy(step, peer, source):
+    def gather_copy(step, part, peer, source):
         return pltpu.make_async_remote_copy(
-            src_ref=newest.at[step],
-            dst_ref=window.at[step, source],
-            send_sem=ag_send.at[step, peer],
-            recv_sem=ag_recv.at[step, source],
+            src_ref=newest.at[step, part],
+            dst_ref=window.at[step, part, source],
+            send_sem=ag_send.at[step, part, peer],
+            recv_sem=ag_recv.at[step, part, source],
             device_id={"row": peer},
             device_id_type=MESH,
         )
 
-    def start_gather(step, value):
-        newest[step] = value
+    def start_gather(step, part, value):
+        newest[step, part] = value
         for peer in row_peers:
-            gather_copy(step, peer, row).start()
-        window[step, row] = value
-
-    def wait_gather(step):
+            gather_copy(step, part, peer, row).start()
+        window[step, part, row] = value
+
+    def wait_gather(step, part):
         for peer in row_peers:
-            gather_copy(step, peer, peer).wait_recv()
-
-    def pair_copy(step, piece):
+            gather_copy(step, part, peer, peer).wait_recv()
+
+    def pair_copy(step, part, piece):
         return pltpu.make_async_remote_copy(
-            src_ref=pair_out.at[step, piece],
-            dst_ref=pair_in.at[step, piece],
-            send_sem=pair_send.at[step, piece],
-            recv_sem=pair_recv.at[step, piece],
+            src_ref=pair_out.at[step, part, piece],
+            dst_ref=pair_in.at[step, part, piece],
+            send_sem=pair_send.at[step, part, piece],
+            recv_sem=pair_recv.at[step, part, piece],
             device_id={"col": partner},
             device_id_type=MESH,
         )
 
-    def pair_top_copy(step):
+    def pair_top_copy(step, part):
         return pltpu.make_async_remote_copy(
-            src_ref=pair_top_out.at[step],
-            dst_ref=pair_top_in.at[step],
-            send_sem=top_send.at[step, n_line],
-            recv_sem=top_recv.at[step, n_line],
+            src_ref=pair_top_out.at[step, part],
+            dst_ref=pair_top_in.at[step, part],
+            send_sem=top_send.at[step, part, n_line],
+            recv_sem=top_recv.at[step, part, n_line],
             device_id={"col": partner},
             device_id_type=MESH,
         )
 
-    def line_copy(step, peer, source):
+    def line_copy(step, part, peer, source):
         return pltpu.make_async_remote_copy(
-            src_ref=line_out.at[step, peer],
-            dst_ref=line_in.at[step, source],
-            send_sem=line_send.at[step, peer],
-            recv_sem=line_recv.at[step, source],
+            src_ref=line_out.at[step, part, peer],
+            dst_ref=line_in.at[step, part, source],
+            send_sem=line_send.at[step, part, peer],
+            recv_sem=line_recv.at[step, part, source],
             device_id={"col": peer * PAIR + side},
             device_id_type=MESH,
         )
 
-    def line_top_copy(step, peer, source):
+    def line_top_copy(step, part, peer, source):
         return pltpu.make_async_remote_copy(
-            src_ref=line_top_out.at[step],
-            dst_ref=line_top_in.at[step, source],
-            send_sem=top_send.at[step, peer],
-            recv_sem=top_recv.at[step, source],
+            src_ref=line_top_out.at[step, part],
+            dst_ref=line_top_in.at[step, part, source],
+            send_sem=top_send.at[step, part, peer],
+            recv_sem=top_recv.at[step, part, source],
             device_id={"col": peer * PAIR + side},
             device_id_type=MESH,
         )
 
-    def exchange_copy(peer, source):
+    def exchange_copy(part, peer, source):
         return pltpu.make_async_remote_copy(
-            src_ref=outgoing.at[peer],
-            dst_ref=arrived.at[source],
-            send_sem=ex_send.at[peer],
-            recv_sem=ex_recv.at[source],
+            src_ref=outgoing.at[part, peer],
+            dst_ref=arrived.at[part, source],
+            send_sem=ex_send.at[part, peer],
+            recv_sem=ex_recv.at[part, source],
             device_id={"row": peer},
             device_id_type=MESH,
         )
 
-    def window_of(step):
-        return window[step].reshape(depth, reals)
+    def window_of(step, part):
+        return window[step, part].reshape(depth, wide)
+
+    lanes = [slice(part * wide, (part + 1) * wide) for part in range(PARTS)]
 
     def lag_share(step, first, last):
         low = (first + 1 - step) * depth
@@ -301,7 +302,10 @@
         base_force[step] = acc[...].T.reshape(n_line, PAIR, slab, reals)
 
     get_v.wait()
-    start_gather(0, v[...].astype(jnp.bfloat16))
+    for part in range(PARTS):
+        start_gather(0, part, v[:, lanes[part]].astype(jnp.bfloat16))
+    get_state = [fetch(x_hbm, x), fetch(a_hbm, a), fetch(exc_hbm, exc), fetch(solve_hbm, solve), fetch(stiff_hbm, stiff)]
+    get_tables = [fetch(owned_hbm, owned), fetch(links_hbm, links), fetch(arms_hbm, arms)]
     get_first.wait()
     k_t[...] = kern[0].reshape(depth, block).T.reshape(n_line, PAIR, slab, depth)
     for index, (first, last) in enumerate(groups):
@@ -312,64 +316,65 @@
         add_lags(0, index, index == 0)
     close_lags(0)
 
-    def half_force(step, which):
-        now = dot(k_t[:, which].reshape(half, depth), window_of(step))
-        return base_force[step, :, which] + now.reshape(n_line, slab, reals)
-
-    def send_force(step):
-        wait_gather(step)
-        theirs = half_force(step, other)
+    def half_force(step, part, which):
+        now = dot(k_t[:, which].reshape(half, depth), window_of(step, part))
+        return base_force[step, :, which][:, :, lanes[part]] + now.reshape(n_line, slab, wide)
+
+    def send_force(step, part):
+        wait_gather(step, part)
+        theirs = half_force(step, part, other)
         top = largest(theirs)
-        pair_top_out[step] = top
-        pair_top_copy(step).start()
-        own_force[...] = theirs
+        pair_top_out[step, part] = top
+        pair_top_copy(step, part).start()
+        own_force[part] = theirs
         for piece in [*line_peers, line]:
-            pair_out[step, piece] = coded(own_force[piece], top)
-            pair_copy(step, piece).start()
-        mine = half_force(step, side)
-        own_force[...] = mine
+            pair_out[step, part, piece] = coded(own_force[part, piece], top)
+            pair_copy(step, part, piece).start()
+        mine = half_force(step, part, side)
+        own_force[part] = mine
         return largest(mine)
 
-    def pass_on(step, own_top, early, late):
-        for filler in early:
-            filler()
-        pair_top_copy(step).wait_recv()
-        top_in = pair_top_in[step]
+    def pass_on(step, part, own_top):
+        pair_top_copy(step, part).wait_recv()
+        top_in = pair_top_in[step, part]
         top = own_top + top_in
-        line_top_out[step] = top
+        line_top_out[step, part] = top
         for peer in line_peers:
-            line_top_copy(step, peer, line).start()
+            pair_copy(step, part, peer).wait_recv()
+            share = decoded(pair_in[step, part, peer], top_in)
+            line_out[step, part, peer] = coded(own_force[part, peer] + share, top)
+            line_copy(step, part, peer, line).start()
+            line_top_copy(step, part, peer, line).start()
+        pair_copy(step, part, line).wait_recv()
+        own_force[part, line] = own_force[part, line] + decoded(pair_in[step, part, line], top_in)
+
+    def collect(step, part):
+        total = own_force[part, line]
         for peer in line_peers:
-            pair_copy(step, peer).wait_recv()
-            line_out[step, peer] = coded(own_force[peer] + decoded(pair_in[step, peer], top_in), top)
-            line_copy(step, peer, line).start()
-        pair_copy(step, line).wait_recv()
-        total = own_force[line] + decoded(pair_in[step, line], top_in)
-        own_force[line] = total
-        for filler in late:
-            filler()
-        total = own_force[line]
-        for peer in line_peers:
-            line_top_copy(step, peer, peer).wait_recv()
-            line_copy(step, peer, peer).wait_recv()
-            total = total + decoded(line_in[step, peer], line_top_in[step, peer])
+            line_top_copy(step, part, peer, peer).wait_recv()
+            line_copy(step, part, peer, peer).wait_recv()
+            total = total + decoded(line_in[step, part, peer], line_top_in[step, part, peer])
         return total
 
-    own_top = send_force(0)
+    own_top = [send_force(0, part) for part in range(PARTS)]
 
     for copy in get_state:
         copy.wait()
-    solve_left = left_pieces(block_diagonal(solve, modules))
+    solve_full = block_diagonal(solve, modules)
+    solve_left = left_pieces(solve_full)
     stiff_left = left_pieces(block_diagonal(stiff, modules))
 
     def newest_past(step):
-        past_t[:, (1 - step) * depth : (2 - step) * depth] = window_of(step).T
+        for part in range(PARTS):
+            past_t[lanes[part], (1 - step) * depth : (2 - step) * depth] = window_of(step, part).T
 
     def tables():
         for copy in get_tables:
             copy.wait()
         route = routing_matrix(owned[...], grid_index * modules, modules).astype(jnp.bfloat16)
-        routing[...] = jnp.concatenate([route, route, route], axis=1)
+        start = predicted_last[...]
+        base_out[...] = dot(jnp.concatenate([route, route, route], axis=1), jnp.concatenate(pieces(start, 3), axis=0))
+        weights[...] = left_pieces(dot(route.astype(jnp.float32), solve_full, EXACT))
         forms = dot(
             gap_matrix(links, arms, grid_index * modules * POINTS, modules),
             choice_matrix(owned[...], row, col, n_col * modules, modules),
@@ -384,7 +389,7 @@
         ]
 
     fillers = [fill_lags(1), fill_lags(2), [tables]]
-    early_ends, late_ends = (0, 1, 0), (3, 4, 1)
+    early_ends, late_ends = (0, 1, 0), (2, 3, 1)
 
 
     displacement, velocity, acceleration = x[...], v[...], a[...]
@@ -392,41 +397,58 @@
         predicted = displacement + DT * velocity + QUARTER * acceleration
         known = dot(solve_left, right_pieces(exc[step] - dot(stiff_left, right_pieces(predicted))))
         drift = velocity + 0.5 * DT * (acceleration + known)
+        if step + 1 == STEPS:
+            predicted_last[...] = predicted + QUARTER * known
         if step + 1 < STEPS:
             newest_past(step)
         work = fillers[step]
-        total = pass_on(step, own_top, work[: early_ends[step]], work[early_ends[step] : late_ends[step]])
-        answer = dot(solve_left, right_pieces(total))
-        velocity = drift - 0.5 * DT * answer
+        for filler in work[: early_ends[step]]:
+            filler()
+        for part in range(PARTS):
+            pass_on(step, part, own_top[part])
+        for filler in work[early_ends[step] : late_ends[step]]:
+            filler()
+        answers = []
+        for part in range(PARTS):
+            total = right_pieces(collect(step, part))
+            if step + 1 == STEPS:
+                leaving = base_out[:, lanes[part]] - QUARTER * dot(weights[...], total)
+                outgoing[part] = leaving.reshape(n_row, LANE_ROWS, wide)
+                for peer in row_peers:
+                    exchange_copy(part, peer, row).start()
+                arrived[part, row] = outgoing[part, row]
+                v_out[:, lanes[part]] = drift[:, lanes[part]] - 0.5 * DT * dot(solve_left, total)
+            else:
+                answers.append(dot(solve_left, total))
+                newer = drift[:, lanes[part]] - 0.5 * DT * answers[part]
+                start_gather(step + 1, part, newer.astype(jnp.bfloat16))
         if step + 1 < STEPS:
-            start_gather(step + 1, velocity.astype(jnp.bfloat16))
-        acceleration = known - answer
-        displacement = predicted + QUARTER * acceleration
-        for filler in work[late_ends[step] :]:
-            filler()
-        if step + 1 < STEPS:
-            own_top = send_force(step + 1)
-
-    leaving = dot(routing[...], jnp.concatenate(pieces(displacement, 3), axis=0))
-    outgoing[...] = leaving.reshape(n_row, LANE_ROWS, reals)
-    for peer in row_peers:
-        exchange_copy(peer, row).start()
-    arrived[row] = outgoing[row]
-    v_out[...] = velocity
-    for step in range(STEPS):
+            answer = jnp.concatenate(answers, axis=1)
+            velocity = drift - 0.5 * DT * answer
+            acceleration = known - answer
+            displacement = predicted + QUARTER * acceleration
+            for filler in work[late_ends[step] :]:
+                filler()
+            own_top = [send_force(step + 1, part) for part in range(PARTS)]
+
+    for part in range(PARTS):
+        for step in range(STEPS):
+            for peer in row_peers:
+                gather_copy(step, part, peer, row).wait_send()
+            pair_top_copy(step, part).wait_send()
+            for piece in [*line_peers, line]:
+                pair_copy(step, part, piece).wait_send()
+            for peer in line_peers:
+                line_top_copy(step, part, peer, line).wait_send()
+                line_copy(step, part, peer, line).wait_send()
+    for part in range(PARTS):
         for peer in row_peers:
-            gather_copy(step, peer, row).wait_send()
-        pair_top_copy(step).wait_send()
-        for piece in [*line_peers, line]:
-            pair_copy(step, piece).wait_send()
-        for peer in line_peers:
-            line_top_copy(step, peer, line).wait_send()
-            line_copy(step, peer, line).wait_send()
-    for peer in row_peers:
-        exchange_copy(peer, peer).wait_recv()
-    deck_out[...] = dot(gaps[...], right_pieces(arrived[...].reshape(n_row * LANE_ROWS, reals)))
-    for peer in row_peers:
-        exchange_copy(peer, row).wait_send()
+            exchange_copy(part, peer, peer).wait_recv()
+        everything = right_pieces(arrived[part].reshape(n_row * LANE_ROWS, wide))
+        deck_out[:, lanes[part]] = dot(gaps[...], everything)
+    for part in range(PARTS):
+        for peer in row_peers:
+            exchange_copy(part, peer, row).wait_send()
 
 
 def body(
@@ -439,6 +461,7 @@
     block = kernel.shape[3]
     depth = n_row * slab
     n_line = n_col // PAIR
+    wide = reals // PARTS
     points = modules * POINTS * 3
     arrivals = n_row * LANE_ROWS
     anywhere = pl.BlockSpec(memory_space=pl.ANY)
@@ -472,32 +495,34 @@
             vm((n_line, PAIR, slab, depth), bf16),
             vm((reals, block), fp32),
             vm((STEPS, n_line, PAIR, slab, reals), fp32),
-            vm((n_line, slab, reals), fp32),
-            vm((STEPS, slab, reals), bf16),
-            vm((STEPS, n_row, slab, reals), bf16),
-            vm((STEPS, n_line, slab, reals), i16),
-            vm((STEPS, n_line, slab, reals), i16),
-            vm((STEPS, n_line, slab, reals), i16),
-            vm((STEPS, n_line, slab, reals), i16),
-            vm((n_row, LANE_ROWS, reals), fp32),
-            vm((n_row, LANE_ROWS, reals), fp32),
+            vm((PARTS, n_line, slab, wide), fp32),
+            vm((STEPS, PARTS, slab, wide), bf16),
+            vm((STEPS, PARTS, n_row, slab, wide), bf16),
+            vm((STEPS, PARTS, n_line, slab, wide), i16),
+            vm((STEPS, PARTS, n_line, slab, wide), i16),
+            vm((STEPS, PARTS, n_line, slab, wide), i16),
+            vm((STEPS, PARTS, n_line, slab, wide), i16),
+            vm((PARTS, n_row, LANE_ROWS, wide), fp32),
+            vm((PARTS, n_row, LANE_ROWS, wide), fp32),
             vm((points, 4 * arrivals), bf16),
-            vm((arrivals, 3 * slab), bf16),
-            vm((STEPS, 1, reals), fp32),
-            vm((STEPS, 1, reals), fp32),
-            vm((STEPS, 1, reals), fp32),
-            vm((STEPS, n_line, 1, reals), fp32),
+            vm((arrivals, 4 * slab), bf16),
+            vm((arrivals, reals), fp32),
+            vm((slab, reals), fp32),
+            vm((STEPS, PARTS, 1, wide), fp32),
+            vm((STEPS, PARTS, 1, wide), fp32),
+            vm((STEPS, PARTS, 1, wide), fp32),
+            vm((STEPS, PARTS, n_line, 1, wide), fp32),
             sems((32,)),
-            sems((STEPS, n_row)),
-            sems((STEPS, n_row)),
-            sems((STEPS, n_line)),
-            sems((STEPS, n_line)),
-            sems((STEPS, n_line)),
-            sems((STEPS, n_line)),
-            sems((STEPS, n_line + 1)),
-            sems((STEPS, n_line + 1)),
-            sems((n_row,)),
-            sems((n_row,)),
+            sems((STEPS, PARTS, n_row)),
+            sems((STEPS, PARTS, n_row)),
+            sems((STEPS, PARTS, n_line)),
+            sems((STEPS, PARTS, n_line)),
+            sems((STEPS, PARTS, n_line)),
+            sems((STEPS, PARTS, n_line)),
+            sems((STEPS, PARTS, n_line + 1)),
+            sems((STEPS, PARTS, n_line + 1)),
+            sems((PARTS, n_row)),
+            sems((PARTS, n_row)),
         ],
         compiler_params=pltpu.CompilerParams(
             collective_id=0, has_side_effects=True, vmem_limit_bytes=56 * 1024 * 1024

time: 62.3 us -> 61.1 us (0.981)
  Pallas kernels: 60.2 us -> 58.8 us
    pallas_call x1, Pallas kernels: 60.2 us -> 58.8 us  [body(): pl.pallas_call(functools.partial(steps_kernel, n_row, n_col, lags, groups...]
where the time goes in v4:
time: 61.1 us; the launch traced here: 60.8 us
  Pallas kernels  58.8 us (96%)
  local copies, waits for them, and re-layouts  1.37 us (2%)
  between operations  0.64 us (1%)
    pallas_call x1, Pallas kernels, body(): pl.pallas_call(functools.partial(steps_kernel, n_row, n_col, lags, groups...  58.8 us
    unnamed x2, local copies, waits for them, and re-layouts  1.37 us

profile of v4, /device:TPU:2, one launch (start us, length us, event | category | flops | bytes accessed | tf_op | source)
XLA Modules:
  0.0 60.8 jit_solution(17378728101088501491)
XLA Ops:
  0.6 58.8 %shard_map.122 = (f32[48,256]{1,0:T(8,128)S(1)}, f32[384,256]{1,0:T(8,128)S(1)}) custom-call(bf16[16,8,48,768]{3,2,1,0:T(8,128)(2,1)} %kernel_hbm.1, bf16[15,8,48,256]{3,2,1,0:T(8,128)(2,1)} %history_hbm.1, f32[48,256]{1,0:T(8,128)} %x_hbm.1, f32[48,256]{1,0:T(8,128)} %v_hbm.1, f32[48,256]{1,0:T(8,128)} %a_hbm.1, f32[3,48,256]{2,1,0:T(8,128)} %exc_hbm.1, ...), custom_call_target="tpu_custom_call" | custom-call | tf_op jit(solution)/shard_map/pallas_call | solution.py:477
  59.4 0.6 %copy.15 = f32[48,256]{1,0:T(8,128)} copy(f32[48,256]{1,0:T(8,128)S(1)} %get-tuple-element.6) | data formatting | bytes 98304
  60.1 0.7 %copy.16 = f32[8,16,3,256]{3,1,2,0:T(8,128)} copy(f32[8,16,3,256]{3,1,2,0:T(8,128)S(1)} %bitcast.7) | data formatting | bytes 786432

commit v5 on v4

--- a/solution.py
+++ b/solution.py
@@ -199,7 +199,7 @@
         for d in (2, 1, 3, 0)
         if t or d
     ]
-    far_first = sorted(range(1, n_line), key=lambda d: -min(d, n_line - d))
+    far_first = sorted(range(1, n_line), key=lambda d: (-min(d, n_line - d), -d))
     line_peers = [lax.rem(line + d, n_line) for d in far_first]
 
     barrier = pltpu.get_barrier_semaphore()
@@ -358,17 +358,11 @@
 
     own_top = [send_force(0, part) for part in range(PARTS)]
 
-    for copy in get_state:
-        copy.wait()
-    solve_full = block_diagonal(solve, modules)
-    solve_left = left_pieces(solve_full)
-    stiff_left = left_pieces(block_diagonal(stiff, modules))
-
     def newest_past(step):
         for part in range(PARTS):
             past_t[lanes[part], (1 - step) * depth : (2 - step) * depth] = window_of(step, part).T
 
-    def tables():
+    def tables(solve_full):
         for copy in get_tables:
             copy.wait()
         route = routing_matrix(owned[...], grid_index * modules, modules).astype(jnp.bfloat16)
@@ -388,25 +382,28 @@
             functools.partial(close_lags, step)
         ]
 
-    fillers = [fill_lags(1), fill_lags(2), [tables]]
-    early_ends, late_ends = (0, 1, 0), (2, 3, 1)
-
-
-    displacement, velocity, acceleration = x[...], v[...], a[...]
+    fillers = [fill_lags(1), fill_lags(2), []]
+    late_ends = (0, 0, 0)
+
+
     for step in range(STEPS):
+        work = fillers[step]
+        for part in range(PARTS):
+            pass_on(step, part, own_top[part])
+        if step == 0:
+            for copy in get_state:
+                copy.wait()
+            solve_full = block_diagonal(solve, modules)
+            solve_left = left_pieces(solve_full)
+            stiff_left = left_pieces(block_diagonal(stiff, modules))
+            displacement, velocity, acceleration = x[...], v[...], a[...]
         predicted = displacement + DT * velocity + QUARTER * acceleration
         known = dot(solve_left, right_pieces(exc[step] - dot(stiff_left, right_pieces(predicted))))
         drift = velocity + 0.5 * DT * (acceleration + known)
         if step + 1 == STEPS:
             predicted_last[...] = predicted + QUARTER * known
-        if step + 1 < STEPS:
-            newest_past(step)
-        work = fillers[step]
-        for filler in work[: early_ends[step]]:
-            filler()
-        for part in range(PARTS):
-            pass_on(step, part, own_top[part])
-        for filler in work[early_ends[step] : late_ends[step]]:
+            tables(solve_full)
+        for filler in work[: late_ends[step]]:
             filler()
         answers = []
         for part in range(PARTS):
@@ -427,6 +424,7 @@
             velocity = drift - 0.5 * DT * answer
             acceleration = known - answer
             displacement = predicted + QUARTER * acceleration
+            newest_past(step)
             for filler in work[late_ends[step] :]:
                 filler()
             own_top = [send_force(step + 1, part) for part in range(PARTS)]

time: 61.1 us -> 61.5 us (level)
  no operation moved by 1% of the time
where the time goes in v5:
time: 61.5 us; the launch traced here: 61.4 us
  Pallas kernels  59.4 us (97%)
  local copies, waits for them, and re-layouts  1.37 us (2%)
  between operations  0.64 us (1%)
    pallas_call x1, Pallas kernels, body(): pl.pallas_call(functools.partial(steps_kernel, n_row, n_col, lags, groups...  59.4 us
    unnamed x2, local copies, waits for them, and re-layouts  1.37 us

profile of v5, /device:TPU:2, one launch (start us, length us, event | category | flops | bytes accessed | tf_op | source)
XLA Modules:
  0.0 61.4 jit_solution(5718759952056967430)
XLA Ops:
  0.6 59.4 %shard_map.122 = (f32[48,256]{1,0:T(8,128)S(1)}, f32[384,256]{1,0:T(8,128)S(1)}) custom-call(bf16[16,8,48,768]{3,2,1,0:T(8,128)(2,1)} %kernel_hbm.1, bf16[15,8,48,256]{3,2,1,0:T(8,128)(2,1)} %history_hbm.1, f32[48,256]{1,0:T(8,128)} %x_hbm.1, f32[48,256]{1,0:T(8,128)} %v_hbm.1, f32[48,256]{1,0:T(8,128)} %a_hbm.1, f32[3,48,256]{2,1,0:T(8,128)} %exc_hbm.1, ...), custom_call_target="tpu_custom_call" | custom-call | tf_op jit(solution)/shard_map/pallas_call | solution.py:475
  60.0 0.6 %copy.15 = f32[48,256]{1,0:T(8,128)} copy(f32[48,256]{1,0:T(8,128)S(1)} %get-tuple-element.6) | data formatting | bytes 98304
  60.6 0.7 %copy.16 = f32[8,16,3,256]{3,1,2,0:T(8,128)} copy(f32[8,16,3,256]{3,1,2,0:T(8,128)S(1)} %bitcast.7) | data formatting | bytes 786432
